TPU v7x, 512 devices: a whole 4x4x16 slice. The times are simulated.
512 devices in a mesh: bunch: 64 (over z, x), dom: 8 (over y, core).
Axes of the slice: x: 4, y: 4, z: 16, core: 2. Of those that a mesh axis runs over, the one named last changes fastest.
Arguments:
- positions: float32 [2, 2, 256, 1024], P(None, None, 'bunch', 'dom'), may hold values from -30 to 30
- slice_index: int32 [2, 256, 1024], P(None, 'bunch', 'dom'), may hold values from 0 to 3
- encounters: int32 [256, 7], P('bunch'), may hold values from 0 to 1, as said below
Outputs:
- fields: float32 [2, 256, 4, 2, 64, 64], P(None, 'bunch')
- particle_kicks: float32 [2, 2, 256, 1024], P(None, None, 'bunch', 'dom')
Inputs may be any that keep to these rules, and one draw needn't show every extreme that they name: `encounters`: among the 4 rows n * 4 to (n + 1) * 4 - 1 that one index of bunch holds, at most 8 entries are 1 and at least 2; in every draw some such block holds exactly 8. In every such block the first row's column 0 and the last row's column 6 are 1.
All inputs are finite; a program needn't handle non-finite values.
Results may differ from a plain program's by a relative error of at most 0.0003.
Values sent between devices are 32-bit elements; how exact they have to be, the bound alone decides.
A program may use at most 128 MiB of HBM per device.

v0:
```python
import jax
import jax.numpy as jnp
import numpy as np
from jax import lax
from jax.sharding import PartitionSpec as P

G = 64
SLICES = 4
R = 3
NOFF = 7
MAXV = 8


CHARGE = 8.0
SOFTEN = 1.0
HIGHEST = lax.Precision.HIGHEST


def shifted(x, axis, by):
    length = lax.axis_size(axis)
    return lax.ppermute(x, axis, [(i, (i + by) % length) for i in range(length)])


def padded(x, sides, width):
    for axis, dim in sides:
        size, length = (lax.axis_size(axis), x.shape[dim])
        up = [(i, (i + 1) % size) for i in range(size)]
        down = [(j, i) for i, j in up]
        last = lax.slice_in_dim(x, length - width, length, axis=dim)
        leading = lax.slice_in_dim(x, 0, width, axis=dim)
        before = lax.ppermute(last, axis, up)
        after = lax.ppermute(leading, axis, down)
        x = jnp.concatenate([before, x, after], axis=dim)
    return x


def tent_weights(coordinate, cell_count):
    centre = 0.5 * (cell_count - 1)
    grid_points = jnp.arange(cell_count, dtype=jnp.float32)
    offset = centre + coordinate[..., None, :] - grid_points[:, None]
    return jnp.maximum(0.0, 1.0 - jnp.abs(offset))


def kernel_space(column, cells_pad, slices, half_range):
    half_cells = cells_pad // 2
    cell_index = jnp.arange(cells_pad, dtype=jnp.int32)
    signed = jnp.where(cell_index < half_cells, cell_index, cell_index - cells_pad).astype(
        jnp.float32
    )
    slice_gap = jnp.arange(2 * slices - 1, dtype=jnp.int32) - (slices - 1)
    column_lead = jnp.asarray(column, jnp.int32) - half_range
    shift_x = (20 * column_lead[..., None] + 4 * slice_gap).astype(jnp.float32)
    shift_y = (3 * column_lead[..., None] + slice_gap).astype(jnp.float32)
    along_x = signed[:, None] + shift_x[..., None, None]
    along_y = signed[None, :] + shift_y[..., None, None]
    spread = along_x * along_x + along_y * along_y + SOFTEN
    return jnp.stack([along_x / spread, along_y / spread], axis=-3)


def dft_tables(length, cell_count):
    row_index = jnp.arange(length, dtype=jnp.int32)
    column_index = jnp.arange(cell_count, dtype=jnp.int32)
    turn_count = row_index[:, None] * column_index[None, :] % length
    phase_angle = turn_count.astype(jnp.float32) * (2.0 * np.pi / length)
    return (jnp.cos(phase_angle), jnp.sin(phase_angle))


def forward_transform(values, cos_table, sin_table):
    real_half = jnp.einsum("kn,...nm->...km", cos_table, values, precision=HIGHEST)
    imag_half = -jnp.einsum("kn,...nm->...km", sin_table, values, precision=HIGHEST)
    real_part = jnp.einsum("...km,lm->...kl", real_half, cos_table, precision=HIGHEST) + jnp.einsum(
        "...km,lm->...kl", imag_half, sin_table, precision=HIGHEST
    )
    imag_part = jnp.einsum("...km,lm->...kl", imag_half, cos_table, precision=HIGHEST) - jnp.einsum(
        "...km,lm->...kl", real_half, sin_table, precision=HIGHEST
    )
    return (real_part, imag_part)


def inverse_transform(real_part, imag_part, cos_table, sin_table):
    length = cos_table.shape[0]
    real_rows = jnp.einsum("kr,...kl->...rl", cos_table, real_part, precision=HIGHEST) - jnp.einsum(
        "kr,...kl->...rl", sin_table, imag_part, precision=HIGHEST
    )
    imag_rows = jnp.einsum("kr,...kl->...rl", cos_table, imag_part, precision=HIGHEST) + jnp.einsum(
        "kr,...kl->...rl", sin_table, real_part, precision=HIGHEST
    )
    result = jnp.einsum("...rl,lq->...rq", real_rows, cos_table, precision=HIGHEST) - jnp.einsum(
        "...rl,lq->...rq", imag_rows, sin_table, precision=HIGHEST
    )
    return result / (length * length)


def gap_lookup():
    return np.arange(SLICES)[:, None] - np.arange(SLICES)[None, :] + SLICES - 1


def field_on_first(kernel_real, kernel_imag, second_real, second_imag, cos_small, sin_small):
    paired_real = kernel_real[gap_lookup()]
    paired_imag = kernel_imag[gap_lookup()]
    on_real = jnp.sum(
        paired_real * second_real[None, :, None] - paired_imag * second_imag[None, :, None], axis=1
    )
    on_imag = jnp.sum(
        paired_real * second_imag[None, :, None] + paired_imag * second_real[None, :, None], axis=1
    )
    return inverse_transform(on_real, on_imag, cos_small, sin_small)


def field_on_second(kernel_real, kernel_imag, first_real, first_imag, cos_small, sin_small):
    paired_real = kernel_real[gap_lookup()]
    paired_imag = kernel_imag[gap_lookup()]
    on_real = jnp.sum(
        -paired_real * first_real[:, None, None] - paired_imag * first_imag[:, None, None], axis=0
    )
    on_imag = jnp.sum(
        paired_imag * first_real[:, None, None] - paired_real * first_imag[:, None, None], axis=0
    )
    return inverse_transform(on_real, on_imag, cos_small, sin_small)


def return_rims(extended, half_range):
    own_count = extended.shape[0] - 2 * half_range
    from_lower = shifted(extended[half_range + own_count :], "bunch", 1)
    from_upper = shifted(extended[:half_range], "bunch", -1)
    own_part = extended[half_range : half_range + own_count]
    own_part = own_part.at[:half_range].add(from_lower)
    own_part = own_part.at[own_count - half_range :].add(from_upper)
    return own_part


def deposit_grids(coord_x, coord_y, labels, scale):
    beams = coord_x.shape[0]
    bunches = coord_x.shape[1]
    slice_ids = jnp.arange(SLICES, dtype=jnp.float32)

    def one_bunch(bundle):
        row_x, row_y, row_labels = bundle
        weight_x = tent_weights(row_x, G)
        weight_y = tent_weights(row_y, G)
        slice_mask = (row_labels[None, :] == slice_ids[:, None]).astype(jnp.float32)
        masked_y = slice_mask[:, None, :] * weight_y[None]
        return jnp.einsum("ip,sjp->sij", weight_x, masked_y, precision=HIGHEST) * scale

    flat_labels = labels.astype(jnp.float32).reshape(beams * bunches, -1)
    grids = lax.map(
        one_bunch,
        (coord_x.reshape(beams * bunches, -1), coord_y.reshape(beams * bunches, -1), flat_labels),
    )
    return grids.reshape(beams, bunches, SLICES, G, G)


def on_device(positions, slice_index, encounters):
    dom_count = lax.axis_size("dom")
    dom_rank = lax.axis_index("dom")
    bunches = positions.shape[2]
    particles = positions.shape[3]
    scale = CHARGE / (particles * dom_count)
    partial_charge = deposit_grids(positions[0], positions[1], slice_index, scale)
    charge = lax.psum(partial_charge, "dom")
    cos_small, sin_small = dft_tables(2 * G, G)
    cos_full, sin_full = dft_tables(2 * G, 2 * G)

    def column_kernel(column):
        kernel_real, kernel_imag = forward_transform(
            kernel_space(column, 2 * G, SLICES, R), cos_full, sin_full
        )
        return (kernel_real, kernel_imag)

    partner_charge = padded(charge[1], (("bunch", 0),), R)
    live_slots = encounters.reshape(-1)
    live_rank = jnp.cumsum(live_slots) - 1
    slot_index = jnp.arange(live_slots.shape[0], dtype=jnp.int32)
    capacity = MAXV // dom_count
    near_start = jnp.zeros((bunches, SLICES, 2, G, G), jnp.float32)
    far_start = jnp.zeros((bunches + 2 * R, SLICES, 2, G, G), jnp.float32)

    def solve_one(list_position, totals):
        near_fields, far_fields = totals
        wanted = list_position * dom_count + dom_rank
        slot_hits = ((live_rank == wanted) & (live_slots > 0)).astype(jnp.int32)
        chosen = jnp.sum(slot_hits * slot_index)
        active = jnp.sum(slot_hits).astype(jnp.float32)
        bunch_local = chosen // NOFF
        column = chosen % NOFF
        kernel_real, kernel_imag = column_kernel(column)
        own_charge = lax.dynamic_index_in_dim(charge[0], bunch_local, 0, False)
        other_charge = lax.dynamic_index_in_dim(partner_charge, bunch_local + column, 0, False)
        first_real, first_imag = forward_transform(own_charge, cos_small, sin_small)
        second_real, second_imag = forward_transform(other_charge, cos_small, sin_small)
        on_first = field_on_first(
            kernel_real, kernel_imag, second_real, second_imag, cos_small, sin_small
        )
        on_second = field_on_second(
            kernel_real, kernel_imag, first_real, first_imag, cos_small, sin_small
        )
        near_fields = near_fields.at[bunch_local].add(active * on_first)
        far_fields = far_fields.at[bunch_local + column].add(active * on_second)
        return (near_fields, far_fields)

    near_fields, far_fields = lax.fori_loop(0, capacity, solve_one, (near_start, far_start))
    near_total, extended = lax.psum((near_fields, far_fields), "dom")
    far_total = return_rims(extended, R)
    fields = jnp.stack([near_total, far_total])
    weight_x = tent_weights(positions[0], G)
    weight_y = tent_weights(positions[1], G)
    slice_ids = jnp.arange(SLICES, dtype=jnp.int32)
    slice_mask = (slice_index[:, :, None, :] == slice_ids[:, None]).astype(jnp.float32)
    particle_kicks = jnp.zeros((2, 2, bunches, particles), jnp.float32)
    for slice_number in range(SLICES):
        sampled = jnp.einsum(
            "bncij,bnjp->bncip", fields[:, :, slice_number], weight_y, precision=HIGHEST
        )
        values = jnp.einsum("bnip,bncip->cbnp", weight_x, sampled, precision=HIGHEST)
        particle_kicks = particle_kicks + slice_mask[None, :, :, slice_number] * values
    return (fields, particle_kicks)


def solution(mesh):
    placed = (P(None, None, "bunch", "dom"), P(None, "bunch", "dom"), P("bunch", None))
    return jax.shard_map(
        on_device,
        mesh=mesh,
        in_specs=placed,
        out_specs=(P(None, "bunch", None, None, None, None), P(None, None, "bunch", "dom")),
        check_vma=False,
    )
```

profile of v0, /device:TPU:1, one launch (start us, length us, event | category | flops | bytes accessed | tf_op | source)
XLA Modules:
  0.0 251.9 jit_solution(16378013754210475718)
XLA Ops:
  7.2 0.7 add_bitcast_fusion.1
  7.9 0.7 convert_element_type.117
  8.6 7.9 %while.21 = (s32[]{:T(128)}, f32[8,4,64,64]{2,3,1,0:T(8,128)}, f32[8,128]{1,0:T(8,128)S(1)}, f32[8,128]{1,0:T(8,128)S(1)}, f32[8,128]{1,0:T(8,128)S(1)}, /*index=5*/s32[]{:T(128)}) while((s32[]{:T(128)}, f32[8,4,64,64]{2,3,1,0:T(8,128)}, f32[8,128]{1,0:T(8,128)S(1)}, f32[8,128]{1,0:T(8,128)S(1)}, f32[8,128]{1,0:T(8,128)S(1)}, ...), condition=%wide.region_4.5_spmd.clone, body=%wide.region_3.4_spmd.clone.sunk | while | flops 25281792 | bytes 205901 | solution.py:146
  8.7 0.9 fusion.356
  9.7 0.9 fusion.356
  10.7 0.9 fusion.356
  11.7 0.9 fusion.356
  12.7 0.9 fusion.356
  13.7 0.9 fusion.356
  14.7 0.9 fusion.356
  15.6 0.9 fusion.356
  17.0 0.6 convert_reduce_fusion
  20.0 1.1 fusion.24
  21.2 1.1 convolution_bitcast_fusion
  22.3 1.7 fusion.93
  24.1 2.6 %fusion.95 = f32[7,2,128,128]{3,2,1,0:T(8,128)} fusion(f32[7,2,128,128]{2,3,1,0:T(8,128)S(1)} %convolution_bitcast_fusion), kind=kOutput, calls=%fused_computation.148 | convolution fusion | flops 352550912 | bytes 1835008 | tf_op jit(solution)/shard_map/while/body/eval_jaxpr/...km,lm->...kl/dot_general | solution.py:71
  26.7 1.7 convolution_subtract_fusion
  28.5 0.7 gather_fusion.1
  29.2 3.2 %convolution_add_fusion = f32[7,2,128,128]{3,2,1,0:T(8,128)S(1)} fusion(f32[7,2,128,128]{3,2,1,0:T(8,128)} %fusion.95, f32[7,2,128,128]{2,3,1,0:T(8,128)} %copy-done.2), kind=kOutput, calls=%fused_computation.45 | convolution fusion | flops 352780288 | bytes 2752512 | tf_op jit(solution)/shard_map/while/body/eval_jaxpr/...km,lm->...kl/dot_general | solution.py:71
  32.4 2.0 gather_fusion
  35.2 0.6 and_reduce_fusion
  35.9 62.5 %all-reduce.4.cloned.1.call-done = f32[2,4,4,64,64]{3,4,2,1,0:T(8,128)} async-done(((f32[2,4,4,64,64]{3,4,2,1,0:T(8,128)}), f32[2,4,4,64,64]{3,4,2,1,0:T(8,128)}) %all-reduce.4.cloned.1.call-update) | async-done | bytes 524304 | tf_op jit(solution)/shard_map/psum | solution.py:160
  98.3 1.4 slice_bitcast_fusion
  100.6 2.7 %collective-permute-start = (f32[3,4,64,64]{2,3,1,0:T(8,128)S(1)}, f32[3,4,64,64]{2,3,1,0:T(8,128)S(1)}, u32[]{:S(2)}, u32[]{:S(2)}) collective-permute-start(f32[3,4,64,64]{2,3,1,0:T(8,128)S(1)} %get-tuple-element.194), channel_id=1, source_target_pairs={{0,8},{8,16},{16,24},{24,32},{32,40},{40,48},{48,56},{56,64},{64,7... | collective-permute-start | bytes 589832 | tf_op jit(solution)/shard_map/ppermute | solution.py:31
  103.3 6.8 %collective-permute-start.1 = (f32[3,4,64,64]{2,3,1,0:T(8,128)S(1)}, f32[3,4,64,64]{2,3,1,0:T(8,128)S(1)}, u32[]{:S(2)}, u32[]{:S(2)}) collective-permute-start(f32[3,4,64,64]{2,3,1,0:T(8,128)S(1)} %get-tuple-element.193), channel_id=1, source_target_pairs={{8,0},{16,8},{24,16},{32,24},{40,32},{48,40},{56,48},{64,56},{72,6... | collective-permute-start | bytes 589832 | tf_op jit(solution)/shard_map/ppermute | solution.py:32
  110.8 0.6 fusion.128
  111.4 0.6 convolution_add_fusion.2
  112.0 0.6 convolution_subtract_fusion.3
  112.7 0.7 subtract_reduce_fusion
  116.2 1.9 broadcast_in_dim.65
  118.0 1.9 fusion.44
  120.8 0.6 fusion.135
  121.4 0.6 fusion.133
  122.7 0.6 convolution_subtract_fusion.6
  125.7 0.8 fusion.38
  127.1 1.1 fusion.41
  128.2 1.0 copy-done.4
  129.3 84.8 %all-reduce.6.cloned.1.call-done = (f32[10,4,2,64,64]{4,3,2,1,0:T(8,128)}, f32[1,4,4,2,64,64]{5,4,3,2,1,0:T(8,128)}) async-done(((f32[10,4,2,64,64]{4,3,2,1,0:T(8,128)}, f32[1,4,4,2,64,64]{5,4,3,2,1,0:T(8,128)}), (f32[10,4,2,64,64]{4,3,2,1,0:T(8,128)}, f32[1,4,4,2,64,64]{5,4,3,2,1,0:T(8,128)})) %all-reduce.6.cloned.1.call-update) | async-done | bytes 1835024 | tf_op jit(solution)/shard_map/psum | solution.py:202
  214.1 1.6 fusion.318
  215.7 3.1 %collective-permute-start.2 = (f32[3,4,2,64,64]{4,3,2,1,0:T(8,128)S(1)}, f32[3,4,2,64,64]{4,3,2,1,0:T(8,128)S(1)}, u32[]{:S(2)}, u32[]{:S(2)}) collective-permute-start(f32[3,4,2,64,64]{4,3,2,1,0:T(8,128)S(1)} %get-tuple-element.192), channel_id=1, source_target_pairs={{0,8},{8,16},{16,24},{24,32},{32,40},{40,48},{48,56},{56,64},{64,7... | collective-permute-start | bytes 1179656 | tf_op jit(solution)/shard_map/ppermute | solution.py:21
  218.9 6.6 %collective-permute-start.3 = (f32[3,4,2,64,64]{4,3,2,1,0:T(8,128)S(1)}, f32[3,4,2,64,64]{4,3,2,1,0:T(8,128)S(1)}, u32[]{:S(2)}, u32[]{:S(2)}) collective-permute-start(f32[3,4,2,64,64]{4,3,2,1,0:T(8,128)S(1)} %get-tuple-element.191), channel_id=1, source_target_pairs={{0,504},{8,0},{16,8},{24,16},{32,24},{40,32},{48,40},{56,48},{64,5... | collective-permute-start | bytes 1179656 | tf_op jit(solution)/shard_map/ppermute | solution.py:21
  225.6 13.4 %collective-permute-done.2 = f32[3,4,2,64,64]{4,3,2,1,0:T(8,128)S(1)} collective-permute-done((f32[3,4,2,64,64]{4,3,2,1,0:T(8,128)S(1)}, f32[3,4,2,64,64]{4,3,2,1,0:T(8,128)S(1)}, u32[]{:S(2)}, u32[]{:S(2)}) %collective-permute-start.2) | collective-permute-done | bytes 393248 | tf_op jit(solution)/shard_map/ppermute | solution.py:21
  239.1 0.7 collective-permute-done.3
  240.3 0.7 fusion.32
  240.9 0.7 fusion.31
  241.6 0.7 fusion.30
  242.3 0.7 fusion.29
  243.0 1.5 pad_maximum_fusion
  (99 shorter events, 11.4 us)
Async XLA Ops:
  7.2 9.5 %copy-start.7 = (s32[4,7]{1,0:T(4,128)S(1)}, s32[4,7]{1,0:T(4,128)}, u32[]{:S(2)}) copy-start(s32[4,7]{1,0:T(4,128)} %param.23) | copy-start | bytes 340
  7.2 91.2 %all-reduce.4.cloned.1.call-start = ((), (), s32[]{:S(2)}) async-start(), calls=%async_computation | async-start | bytes 2097152 | tf_op jit(solution)/shard_map/psum | solution.py:160
  16.6 197.5 %all-reduce.6.cloned.1.call-start = ((), (), s32[]{:S(2)}) async-start(), calls=%async_computation.1 | async-start | bytes 7340032 | tf_op jit(solution)/shard_map/psum | solution.py:202
  21.2 5.6 %copy-start.2 = (f32[7,2,128,128]{2,3,1,0:T(8,128)}, f32[7,2,128,128]{2,3,1,0:T(8,128)S(1)}, u32[]{:S(2)}) copy-start(f32[7,2,128,128]{2,3,1,0:T(8,128)S(1)} %fusion.24) | copy-start | bytes 2752516
  24.1 4.4 %copy-start.8 = (s32[16]{0:T(128)S(1)}, s32[16]{0:T(128)}, u32[]{:S(2)}) copy-start(s32[16]{0:T(128)} %constant.255) | copy-start | bytes 196
  32.4 2.9 %copy-start.9 = (s32[5]{0:T(128)S(1)}, s32[5]{0:T(128)}, u32[]{:S(2)}) copy-start(s32[5]{0:T(128)} %constant.233.clone.1) | copy-start | bytes 64
  32.4 2.8 %copy-start.10 = (s32[5]{0:T(128)S(1)}, s32[5]{0:T(128)}, u32[]{:S(2)}) copy-start(s32[5]{0:T(128)} %constant.246.clone.1) | copy-start | bytes 64
  98.3 2.2 copy-start.5
  99.7 13.0 %copy-start.1 = (f32[16,2,128,128]{3,2,1,0:T(8,128)S(1)}, f32[16,2,128,128]{3,2,1,0:T(8,128)}, u32[]{:S(2)}) copy-start(f32[16,2,128,128]{3,2,1,0:T(8,128)} %gather_fusion) | copy-start | bytes 6291460
  100.6 19.3 %collective-permute-start = (f32[3,4,64,64]{2,3,1,0:T(8,128)S(1)}, f32[3,4,64,64]{2,3,1,0:T(8,128)S(1)}, u32[]{:S(2)}, u32[]{:S(2)}) collective-permute-start(f32[3,4,64,64]{2,3,1,0:T(8,128)S(1)} %get-tuple-element.194), channel_id=1, source_target_pairs={{0,8},{8,16},{16,24},{24,32},{32,40},{40,48},{48,56},{56,64},{64,7... | collective-permute-start | bytes 589832 | tf_op jit(solution)/shard_map/ppermute | solution.py:31
  103.3 16.6 %collective-permute-start.1 = (f32[3,4,64,64]{2,3,1,0:T(8,128)S(1)}, f32[3,4,64,64]{2,3,1,0:T(8,128)S(1)}, u32[]{:S(2)}, u32[]{:S(2)}) collective-permute-start(f32[3,4,64,64]{2,3,1,0:T(8,128)S(1)} %get-tuple-element.193), channel_id=1, source_target_pairs={{8,0},{16,8},{24,16},{32,24},{40,32},{48,40},{56,48},{64,56},{72,6... | collective-permute-start | bytes 589832 | tf_op jit(solution)/shard_map/ppermute | solution.py:32
  128.2 1.0 copy-start.4
  129.2 89.6 %copy-start.6 = (s32[2,4,128]{2,1,0:T(4,128)S(1)}, s32[2,4,128]{2,1,0:T(4,128)}, u32[]{:S(2)}) copy-start(s32[2,4,128]{2,1,0:T(4,128)} %param.22) | copy-start | bytes 12292
  214.1 11.4 %copy-start.3 = (f32[10,4,2,64,64]{4,3,2,1,0:T(8,128)S(1)}, f32[10,4,2,64,64]{4,3,2,1,0:T(8,128)}, u32[]{:S(2)}) copy-start(f32[10,4,2,64,64]{4,3,2,1,0:T(8,128)} %get-tuple-element.187) | copy-start | bytes 3932164
  215.7 23.2 %collective-permute-start.2 = (f32[3,4,2,64,64]{4,3,2,1,0:T(8,128)S(1)}, f32[3,4,2,64,64]{4,3,2,1,0:T(8,128)S(1)}, u32[]{:S(2)}, u32[]{:S(2)}) collective-permute-start(f32[3,4,2,64,64]{4,3,2,1,0:T(8,128)S(1)} %get-tuple-element.192), channel_id=1, source_target_pairs={{0,8},{8,16},{16,24},{24,32},{32,40},{40,48},{48,56},{56,64},{64,7... | collective-permute-start | bytes 1179656 | tf_op jit(solution)/shard_map/ppermute | solution.py:21
  218.9 21.0 %collective-permute-start.3 = (f32[3,4,2,64,64]{4,3,2,1,0:T(8,128)S(1)}, f32[3,4,2,64,64]{4,3,2,1,0:T(8,128)S(1)}, u32[]{:S(2)}, u32[]{:S(2)}) collective-permute-start(f32[3,4,2,64,64]{4,3,2,1,0:T(8,128)S(1)} %get-tuple-element.191), channel_id=1, source_target_pairs={{0,504},{8,0},{16,8},{24,16},{32,24},{40,32},{48,40},{56,48},{64,5... | collective-permute-start | bytes 1179656 | tf_op jit(solution)/shard_map/ppermute | solution.py:21
  239.0 1.2 copy-start
Sparse Core Ops, SparseCore 0:
  16.7 81.5 all-reduce.3
  129.3 84.6 all-reduce.5
where the time goes:
time: 255 us; the launch traced here: 252 us
  waiting for transfers between devices  161 us (63%)
  matrix products  37 us (15%)
  starting transfers between devices  19.3 us (8%)
  between operations  17.2 us (7%)
  local copies, waits for them, and re-layouts  9.48 us (4%)
  other arithmetic  7.35 us (3%)
    psum x1, waiting for transfers between devices, on_device(): near_total, extended = lax.psum((near_fields, far_fields), 'dom')  84.8 us
    psum x1, waiting for transfers between devices, on_device(): charge = lax.psum(partial_charge, 'dom')  62.5 us
    ppermute x2, waiting for transfers between devices, shifted(): lax.ppermute(x, axis, [(i, (i + by) % length) for i in range(length)])  14.1 us
    ppermute x2, starting transfers between devices, shifted(): lax.ppermute(x, axis, [(i, (i + by) % length) for i in range(length)])  9.72 us
    dot_general x8, matrix products, one_bunch(): jnp.einsum('ip,sjp->sij', weight_x, masked_y, precision=HIGHEST) * scale  7.42 us
    ppermute x1, starting transfers between devices, padded(): after = lax.ppermute(leading, axis, down)  6.8 us
  transfers between devices with their start and end apart: 6, of which 4 were waited for; matrix products, arithmetic and copies ran while one was open for 10% of the time, Pallas kernels for 0%

commit v1 on v0

v1 whole, which is shorter than its diff:
```python
import functools

import jax
import jax.numpy as jnp
import ml_dtypes
import numpy as np
from jax import lax
from jax.experimental import pallas as pl
from jax.experimental.pallas import tpu as pltpu
from jax.sharding import PartitionSpec as P

G = 64
SLICES = 4
R = 3
NOFF = 7
CHARGE = 8.0
SOFTEN = 1.0

BUN = 4
SRC = BUN + 2 * R
N1 = 152
N2 = 134
ROWS = 80
MESH = pl.DeviceIdType.MESH
BF = jnp.bfloat16
F32 = jnp.float32


def split_table(values):
    high = values.astype(ml_dtypes.bfloat16)
    low = (values - high.astype(np.float64)).astype(ml_dtypes.bfloat16)
    return high, low


@functools.lru_cache(maxsize=None)
def tables(scale):
    line = np.arange(ROWS)
    kx = np.arange(ROWS)
    live_kx = (kx <= N1 // 2).astype(np.float64)
    ky = np.arange(128)
    live_ky = (ky <= N2 // 2).astype(np.float64)

    phase_y = 2.0 * np.pi * (line[:, None] * ky[None, :] % N2) / N2
    along = np.concatenate([np.cos(phase_y) * live_ky, -np.sin(phase_y) * live_ky], axis=1)
    fwd_y = split_table(np.concatenate([along, along], axis=0))

    phase_x = 2.0 * np.pi * (kx[:, None] * line[None, :] % N1) / N1
    cos_x = np.cos(phase_x) * live_kx[:, None]
    sin_x = np.sin(phase_x) * live_kx[:, None]
    high, low = split_table(np.concatenate([cos_x, sin_x], axis=0))
    fwd_x = np.concatenate([high, high, low], axis=1)

    half = np.where((kx == 0) | (kx == N1 // 2), 0.5, 1.0) / (N1 * N2)
    high, low = split_table(np.concatenate([(cos_x * half[:, None]).T, (sin_x * half[:, None]).T], axis=1))
    inv_x = np.concatenate([high, low], axis=0)

    twice = np.where((ky == 0) | (ky == N2 // 2), 1.0, 2.0) * live_ky
    cell = np.arange(128)
    live_cell = (cell < G + SLICES - 1).astype(np.float64)
    phase = 2.0 * np.pi * (ky[:, None] * cell[None, :] % N2) / N2
    back = np.concatenate([np.cos(phase) * twice[:, None], -np.sin(phase) * twice[:, None]], axis=0)
    inv_y = np.concatenate(split_table(back * live_cell[None, :]), axis=1)

    d1 = np.arange(N1)
    d1 = np.where(d1 < N1 // 2, d1, d1 - N1).astype(np.float64)
    d2 = np.arange(N2)
    d2 = np.where(d2 < N2 // 2, d2, d2 - N2).astype(np.float64)
    spectra = np.zeros((NOFF, 2, 2, 2 * ROWS, 128), np.float32)
    rows = np.arange(N1 // 2 + 1)
    for column in range(NOFF):
        along_x = d1[:, None] + 20.0 * (column - R)
        along_y = d2[None, :] + 3.0 * (column - R)
        spread = along_x * along_x + along_y * along_y + SOFTEN
        for part, value in enumerate((along_x / spread, along_y / spread)):
            hat = np.fft.fft2(value)[:, : N2 // 2 + 1] * scale
            for half_index, pick in enumerate((rows, (-rows) % N1)):
                place = slice(half_index * ROWS, half_index * ROWS + rows.size)
                spectra[column, part, 0, place, : N2 // 2 + 1] = hat[pick].real
                spectra[column, part, 1, place, : N2 // 2 + 1] = hat[pick].imag
    return fwd_y + (fwd_x, inv_x, inv_y, spectra)


def exchange_kernel(
    groups, doms,
    pos_any, sl_any, enc_any, g_ref, e_ref,
    pos_ref, sl_ref, enc_ref, block, encs, in_sem, send_sem, esend_sem, recv_sem, erecv_sem,
):
    n = lax.axis_index("bunch")
    me = lax.axis_index("dom")
    loads = [
        pltpu.make_async_copy(src, dst, in_sem.at[k])
        for k, (src, dst) in enumerate(((pos_any, pos_ref), (sl_any, sl_ref), (enc_any, enc_ref)))
    ]
    for load in loads:
        load.start()
    peers = []
    for off in (0, 1, -1):
        for j in range(doms):
            if off == 0 and j == 0:
                continue
            peers.append((off, lax.rem(n + off + groups, groups), lax.rem(me + j, doms)))

    barrier = pltpu.get_barrier_semaphore()
    for _, there, dom in peers:
        pl.semaphore_signal(barrier, inc=1, device_id=(there, dom), device_id_type=MESH)

    for load in loads:
        load.wait()
    centre = 0.5 * (G - 1)
    for beam in range(2):
        gap = sl_ref[beam].astype(F32)
        block[beam * 8 : beam * 8 + 4, :] = (centre + pos_ref[0, beam]) + 4.0 * gap
        block[beam * 8 + 4 : beam * 8 + 8, :] = (centre + pos_ref[1, beam]) + gap
    encs[...] = jnp.zeros_like(encs)
    encs[0:BUN, 0:NOFF] = enc_ref[...]
    pl.semaphore_wait(barrier, len(peers))

    sends = []
    for k, off in enumerate((1, -1)):
        copy = pltpu.make_async_remote_copy(
            src_ref=encs,
            dst_ref=e_ref.at[1 - off],
            send_sem=esend_sem.at[k],
            recv_sem=erecv_sem.at[1 - off],
            device_id=(lax.rem(n + off + groups, groups), me),
            device_id_type=MESH,
        )
        copy.start()
        sends.append(copy)
    for k, (off, there, dom) in enumerate(peers):
        copy = pltpu.make_async_remote_copy(
            src_ref=block,
            dst_ref=g_ref.at[1 - off, me],
            send_sem=send_sem.at[k],
            recv_sem=recv_sem.at[1 - off, me],
            device_id=(there, dom),
            device_id_type=MESH,
        )
        copy.start()
        sends.append(copy)
    mine = pltpu.make_async_copy(block, g_ref.at[1, me], recv_sem.at[1, me])
    mine.start()
    mine_e = pltpu.make_async_copy(encs, e_ref.at[1], erecv_sem.at[1])
    mine_e.start()
    for grp in range(3):
        for d in range(doms):
            pltpu.make_async_copy(block, g_ref.at[grp, d], recv_sem.at[grp, d]).wait()
        pltpu.make_async_copy(encs, e_ref.at[grp], erecv_sem.at[grp]).wait()
    for copy in sends:
        copy.wait_send()


def high_low(values):
    high = values.astype(BF)
    return high, (values - high.astype(F32)).astype(BF)


def mm(a, b):
    return jnp.dot(a, b, preferred_element_type=F32)


def live_lists(enc_ref, order, place, pair_c, pair_p, pair_count):
    flags = []
    for beam in range(2):
        for b in range(BUN):
            row = []
            for c in range(NOFF):
                if beam == 0:
                    row.append(enc_ref[1, b, c])
                else:
                    a = b + c + 1
                    row.append(enc_ref[a // BUN, a % BUN, 2 * R - c])
            flags.append(row)
    count = jnp.int32(0)
    for k in range(2 * SRC + 8):
        order[k] = 0
    for source in range(2 * SRC):
        beam, m = source // SRC, source % SRC
        users = [flags[(1 - beam) * BUN + b][m - b] for b in range(BUN) if 0 <= m - b < NOFF]
        need = users[0]
        for other in users[1:]:
            need = jnp.maximum(need, other)
        order[count] = source
        place[source] = count
        count = count + need
    order[count] = 0
    for target in range(2 * BUN):
        beam, b = target // BUN, target % BUN
        total = jnp.int32(0)
        for c in range(NOFF):
            pair_c[target * 8 + total] = c
            pair_p[target * 8 + total] = place[(1 - beam) * SRC + b + c]
            total = total + flags[target][c]
        pair_count[target] = total
    return count


def solve_kernel(
    doms,
    g_ref, enc_ref, fyh_any, fyl_any, fx_any, ix_any, iy_any, kv_any,
    f_any, kick_ref,
    fyh_ref, fyl_ref, fx_ref, ix_ref, iy_ref, kv, table_sem,
    wx, wy, grids, spec, acc, bh_ref, bl_ref, win,
    order, place, pair_c, pair_p, pair_count, out_sem,
):
    pairs = (
        (fyh_any, fyh_ref), (fyl_any, fyl_ref), (fx_any, fx_ref),
        (kv_any, kv), (ix_any, ix_ref), (iy_any, iy_ref),
    )
    loads = [pltpu.make_async_copy(src, dst, table_sem.at[k]) for k, (src, dst) in enumerate(pairs)]
    for load in loads:
        load.start()

    count = live_lists(enc_ref, order, place, pair_c, pair_p, pair_count)
    line = lax.broadcasted_iota(jnp.int32, (16, 128), 0).astype(F32)
    lines = [line + 16.0 * t for t in range(ROWS // 16)]

    def weights(k, dest_x, dest_y):
        source = order[k]
        beam = source // SRC
        m = source - beam * SRC
        grp = (m + 1) // BUN
        bunch = (m + 1) % BUN
        for coord, dest in ((0, dest_x), (1, dest_y)):
            row = beam * 8 + coord * 4 + bunch
            for d in range(doms):
                at = jnp.broadcast_to(g_ref[grp, d, pl.ds(row, 1), :], (16, 128))
                cols = slice(d * 128, (d + 1) * 128)
                for t in range(ROWS // 16):
                    high, low = high_low(jnp.maximum(0.0, 1.0 - jnp.abs(at - lines[t])))
                    dest[16 * t : 16 * t + 16, cols] = high
                    dest[ROWS + 16 * t : ROWS + 16 * t + 16, cols] = low

    def deposit(src_x, src_y, grid):
        both = lax.dot_general(src_x[...], src_y[...], (((1,), (1,)), ((), ())), preferred_element_type=F32)
        ah, al = high_low(both[:ROWS] + both[ROWS:])
        grid[0] = ah
        grid[1] = al

    def spectra(k, grids):
        ah = [grid[0] for grid in grids]
        al = [grid[1] for grid in grids]
        rows = len(grids) * ROWS
        first = mm(jnp.concatenate(ah + al, axis=0), fyh_ref[...])
        first = first[:rows] + first[rows:] + mm(jnp.concatenate(ah, axis=0), fyl_ref[...])
        for s in range(len(grids)):
            rh, rl = high_low(first[s * ROWS : (s + 1) * ROWS])
            out = mm(fx_ref[...], jnp.concatenate([rh, rl, rh], axis=0))
            cr, ci = out[:ROWS, :128], out[:ROWS, 128:]
            sr, si = out[ROWS:, :128], out[ROWS:, 128:]
            spec[k + s, 0, :ROWS] = cr + si
            spec[k + s, 0, ROWS:] = cr - si
            spec[k + s, 1, :ROWS] = ci - sr
            spec[k + s, 1, ROWS:] = ci + sr

    weights(0, wx[0], wy[0])
    weights(1, wx[1], wy[1])
    for load in loads[:3]:
        load.wait()

    def four_sources(j, _):
        k = 4 * j
        spectra(k, grids[2:])
        for s in range(2):
            deposit(wx[s], wy[s], grids[s])
            weights(k + 2 + s, wx[2 + s], wy[2 + s])
        spectra(k + 2, grids[:2])
        for s in range(2):
            deposit(wx[2 + s], wy[2 + s], grids[2 + s])
            weights(k + 4 + s, wx[s], wy[s])
        return 0

    turns = (count + 3) // 4
    lax.fori_loop(0, turns, four_sources, 0)
    spectra(4 * turns, grids[2:])
    for load in loads[3:]:
        load.wait()

    me = lax.axis_index("dom")
    index = lax.broadcasted_iota(jnp.int32, (ROWS, 128), 0).astype(F32)

    def multiply(target, _):
        acc[target] = jnp.zeros_like(acc[target])

        def partner(j, _):
            c = pair_c[target * 8 + j]
            p = pair_p[target * 8 + j] + 2
            for t in range(2 * ROWS // 16):
                rows = slice(16 * t, 16 * t + 16)
                re = spec[p, 0, rows]
                im = spec[p, 1, rows]
                for part in range(2):
                    kr = kv[c, part, 0, rows]
                    ki = kv[c, part, 1, rows]
                    acc[target, part, 0, rows] += kr * re - ki * im
                    acc[target, part, 1, rows] += kr * im + ki * re
            return 0

        lax.fori_loop(0, pair_count[target], partner, 0)
        return 0

    lax.fori_loop(0, 2 * BUN, multiply, 0)

    def finish(beam, _):
        for b in range(BUN):
            target = beam * BUN + b
            for part in range(2):
                rp, rm = acc[target, part, 0, :ROWS], acc[target, part, 0, ROWS:]
                ip, im = acc[target, part, 1, :ROWS], acc[target, part, 1, ROWS:]
                top = jnp.concatenate([rp + rm, ip + im], axis=1)
                low = jnp.concatenate([im - ip, rp - rm], axis=1)
                dh, dl = high_low(jnp.concatenate([top, low], axis=0))
                first = mm(ix_ref[...], dh)
                bh, bl = high_low(first[:ROWS] + first[ROWS:] + mm(ix_ref[:ROWS], dl))
                bh_ref[b, part * ROWS : (part + 1) * ROWS] = bh
                bl_ref[b, part * ROWS : (part + 1) * ROWS] = bl
        for b in range(BUN):
            wide = mm(bh_ref[b], iy_ref[...])
            field = wide[:, :128] + wide[:, 128:] + mm(bl_ref[b], iy_ref[:, :128])
            for part in range(2):
                for i in range(SLICES):
                    win[beam, b, i, part] = field[part * ROWS + 4 * i : part * ROWS + 4 * i + G, i : i + G]

            x = jnp.broadcast_to(g_ref[1, me, pl.ds(beam * 8 + b, 1), :], (ROWS, 128))
            y = jnp.broadcast_to(g_ref[1, me, pl.ds(beam * 8 + 4 + b, 1), :], (ROWS, 128))
            weight_x = jnp.maximum(0.0, 1.0 - jnp.abs(x - index))
            yh, yl = high_low(jnp.maximum(0.0, 1.0 - jnp.abs(y - index)))
            fh, fl = high_low(field[:, :ROWS])
            first = mm(jnp.concatenate([fh, fl], axis=0), jnp.concatenate([yh, yl], axis=1))
            sampled = first[: 2 * ROWS, :128] + first[2 * ROWS :, :128] + first[: 2 * ROWS, 128:]
            for part in range(2):
                kick_ref[part, beam, b : b + 1, :] = jnp.sum(
                    weight_x * sampled[part * ROWS : (part + 1) * ROWS], axis=0, keepdims=True
                )
        pltpu.make_async_copy(win.at[beam], f_any.at[beam], out_sem.at[beam]).start()
        return 0

    lax.fori_loop(0, 2, finish, 0)
    for beam in range(2):
        pltpu.make_async_copy(win.at[beam], f_any.at[beam], out_sem.at[beam]).wait()


def solve(gathered, enc):
    doms, particles = gathered.shape[1], gathered.shape[3]
    vmem = pl.BlockSpec(memory_space=pltpu.VMEM)
    anywhere = pl.BlockSpec(memory_space=pl.ANY)
    consts = [jnp.asarray(t) for t in tables(CHARGE / (particles * doms))]
    weight = pltpu.VMEM((2 * ROWS, doms * particles), BF)
    return pl.pallas_call(
        functools.partial(solve_kernel, doms),
        out_shape=(
            jax.ShapeDtypeStruct((2, BUN, SLICES, 2, G, G), F32),
            jax.ShapeDtypeStruct((2, 2, BUN, particles), F32),
        ),
        in_specs=[vmem, pl.BlockSpec(memory_space=pltpu.SMEM)] + [anywhere] * 6,
        out_specs=(anywhere, vmem),
        scratch_shapes=[pltpu.VMEM(t.shape, t.dtype) for t in consts] + [
            pltpu.SemaphoreType.DMA((len(consts),)),
            [weight] * 4,
            [weight] * 4,
            [pltpu.VMEM((2, ROWS, 2 * ROWS), BF)] * 4,
            pltpu.VMEM((2 * SRC + 4, 2, 2 * ROWS, 128), F32),
            pltpu.VMEM((2 * BUN, 2, 2, 2 * ROWS, 128), F32),
            pltpu.VMEM((BUN, 2 * ROWS, 256), BF),
            pltpu.VMEM((BUN, 2 * ROWS, 256), BF),
            pltpu.VMEM((2, BUN, SLICES, 2, G, G), F32),
            pltpu.SMEM((2 * SRC + 8,), jnp.int32),
            pltpu.SMEM((2 * SRC,), jnp.int32),
            pltpu.SMEM((2 * BUN * 8,), jnp.int32),
            pltpu.SMEM((2 * BUN * 8,), jnp.int32),
            pltpu.SMEM((2 * BUN,), jnp.int32),
            pltpu.SemaphoreType.DMA((2,)),
        ],
        compiler_params=pltpu.CompilerParams(vmem_limit_bytes=24 * 1024 * 1024),
        name="solve",
    )(gathered, enc, *[pltpu.with_memory_space_constraint(t, pltpu.HBM) for t in consts])


def on_device(positions, slice_index, encounters):
    groups, doms = lax.axis_size("bunch"), lax.axis_size("dom")
    particles = positions.shape[3]
    anywhere = pl.BlockSpec(memory_space=pl.ANY)
    gathered, enc = pl.pallas_call(
        functools.partial(exchange_kernel, groups, doms),
        out_shape=(
            jax.ShapeDtypeStruct((3, doms, 16, particles), F32),
            jax.ShapeDtypeStruct((3, 8, 128), jnp.int32),
        ),
        in_specs=[anywhere] * 3,
        out_specs=(anywhere, anywhere),
        scratch_shapes=[
            pltpu.VMEM(positions.shape, F32),
            pltpu.VMEM(slice_index.shape, jnp.int32),
            pltpu.VMEM(encounters.shape, jnp.int32),
            pltpu.VMEM((16, particles), F32),
            pltpu.VMEM((8, 128), jnp.int32),
            pltpu.SemaphoreType.DMA((3,)),
            pltpu.SemaphoreType.DMA((3 * doms - 1,)),
            pltpu.SemaphoreType.DMA((2,)),
            pltpu.SemaphoreType.DMA((3, doms)),
            pltpu.SemaphoreType.DMA((3,)),
        ],
        compiler_params=pltpu.CompilerParams(
            collective_id=0, has_side_effects=True, vmem_limit_bytes=1024 * 1024
        ),
        name="exchange",
    )(*[pltpu.with_memory_space_constraint(v, pltpu.HBM) for v in (positions, slice_index, encounters)])
    return solve(gathered, enc)


def solution(mesh):
    placed = (P(None, None, "bunch", "dom"), P(None, "bunch", "dom"), P("bunch", None))
    return jax.shard_map(
        on_device,
        mesh=mesh,
        in_specs=placed,
        out_specs=(P(None, "bunch", None, None, None, None), P(None, None, "bunch", "dom")),
        check_vma=False,
    )
```

time: 255 us -> 31.3 us (0.12)
  the two profiles are of different devices: /device:TPU:1 before, /device:TPU:3 now
where the time goes in v1:
time: 31.3 us; the launch traced here: 31.1 us
  Pallas kernels  30.5 us (97%)
  between operations  0.64 us (2%)
    pallas_call x1, Pallas kernels, on_device(): pl.pallas_call(functools.partial(exchange_kernel, groups, doms), out_shap...  19.5 us
    pallas_call x1, Pallas kernels, solve(): pl.pallas_call(functools.partial(solve_kernel, doms), out_shape=(jax.Shap...  11 us

profile of v1, /device:TPU:3, one launch (start us, length us, event | category | flops | bytes accessed | tf_op | source)
XLA Modules:
  0.0 31.1 jit_solution(11185695084402538470)
XLA Ops:
  0.6 19.5 %exchange.1 = (f32[3,8,16,128]{3,2,1,0:T(8,128)S(1)}, s32[3,8,128]{2,1,0:T(8,128)S(1)}) custom-call(f32[2,2,4,128]{3,2,1,0:T(4,128)} %pos_any.1, s32[2,4,128]{2,1,0:T(4,128)} %sl_any.1, s32[4,7]{1,0:T(4,128)} %enc_any.1), custom_call_target="tpu_custom_call" | custom-call | tf_op jit(solution)/shard_map/exchange/pallas_call | solution.py:383
  20.1 11.0 %solve.1 = (f32[2,4,4,2,64,64]{5,4,3,2,1,0:T(8,128)}, f32[2,2,4,128]{3,2,1,0:T(4,128)}) custom-call(f32[3,8,16,128]{3,2,1,0:T(8,128)S(1)} %get-tuple-element.4.g_ref, s32[3,8,128]{2,1,0:T(8,128)S(1)} %get-tuple-element.5.enc_ref, bf16[160,256]{1,0:T(8,128)(2,1)} %constant.12.clone.fyh_any, bf16[160,256]{1,0:T(8,128)(2,1)} %constant.13.clone.fyl_any, ...), custom_call_target="tpu_custom_call" | custom-call | tf_op jit(solution)/shard_map/solve/pallas_call | solution.py:349

commit v2 on v1

v2 whole, which is shorter than its diff:
```python
import functools

import jax
import jax.numpy as jnp
import ml_dtypes
import numpy as np
from jax import lax
from jax.experimental import pallas as pl
from jax.experimental.pallas import tpu as pltpu
from jax.sharding import PartitionSpec as P

G = 64
SLICES = 4
R = 3
NOFF = 7
CHARGE = 8.0
SOFTEN = 1.0

BUN = 4
SRC = BUN + 2 * R
ALWAYS = (SRC, 2 * SRC - 1, R - 1, R + BUN)
N1 = 152
N2 = 134
ROWS = 80
MESH = pl.DeviceIdType.MESH
BF = jnp.bfloat16
F32 = jnp.float32


def split_table(values):
    high = values.astype(ml_dtypes.bfloat16)
    low = (values - high.astype(np.float64)).astype(ml_dtypes.bfloat16)
    return high, low


@functools.lru_cache(maxsize=None)
def tables(scale):
    line = np.arange(ROWS)
    kx = np.arange(ROWS)
    live_kx = (kx <= N1 // 2).astype(np.float64)
    ky = np.arange(128)
    live_ky = (ky <= N2 // 2).astype(np.float64)

    phase_y = 2.0 * np.pi * (line[:, None] * ky[None, :] % N2) / N2
    along = np.concatenate([np.cos(phase_y) * live_ky, -np.sin(phase_y) * live_ky], axis=1)
    high, low = split_table(along)
    fwd_y = np.concatenate([np.concatenate([high, high], axis=0), np.concatenate([low, low], axis=0)], axis=1)

    phase_x = 2.0 * np.pi * (kx[:, None] * line[None, :] % N1) / N1
    cos_x = np.cos(phase_x) * live_kx[:, None]
    sin_x = np.sin(phase_x) * live_kx[:, None]
    high, low = split_table(np.concatenate([cos_x, sin_x], axis=0))
    fwd_x = np.concatenate([high, high, low], axis=1)

    half = np.where((kx == 0) | (kx == N1 // 2), 0.5, 1.0) / (N1 * N2)
    high, low = split_table(np.concatenate([(cos_x * half[:, None]).T, (sin_x * half[:, None]).T], axis=1))
    inv_x = np.concatenate([high, high, low], axis=1)

    twice = np.where((ky == 0) | (ky == N2 // 2), 1.0, 2.0) * live_ky
    cell = np.arange(128)
    live_cell = (cell < G + SLICES - 1).astype(np.float64)
    phase = 2.0 * np.pi * (ky[:, None] * cell[None, :] % N2) / N2
    back = np.concatenate([np.cos(phase) * twice[:, None], -np.sin(phase) * twice[:, None]], axis=0)
    inv_y = np.concatenate(split_table(back * live_cell[None, :]), axis=1)

    d1 = np.arange(N1)
    d1 = np.where(d1 < N1 // 2, d1, d1 - N1).astype(np.float64)
    d2 = np.arange(N2)
    d2 = np.where(d2 < N2 // 2, d2, d2 - N2).astype(np.float64)
    spectra = np.zeros((NOFF, 2, 2, 2 * ROWS, 128), np.float32)
    rows = np.arange(N1 // 2 + 1)
    for column in range(NOFF):
        along_x = d1[:, None] + 20.0 * (column - R)
        along_y = d2[None, :] + 3.0 * (column - R)
        spread = along_x * along_x + along_y * along_y + SOFTEN
        for part, value in enumerate((along_x / spread, along_y / spread)):
            hat = np.fft.fft2(value)[:, : N2 // 2 + 1] * scale
            for half_index, pick in enumerate((rows, (-rows) % N1)):
                place = slice(half_index * ROWS, half_index * ROWS + rows.size)
                spectra[column, part, 0, place, : N2 // 2 + 1] = hat[pick].real
                spectra[column, part, 1, place, : N2 // 2 + 1] = hat[pick].imag
    return fwd_y, fwd_x, inv_x, inv_y, spectra


def exchange_kernel(
    groups, doms,
    pos_any, sl_any, enc_any, g_ref, e_ref,
    pos_ref, sl_ref, enc_ref, block, encs, in_sem, sems,
):
    n = lax.axis_index("bunch")
    me = lax.axis_index("dom")
    loads = [
        pltpu.make_async_copy(src, dst, in_sem.at[k])
        for k, (src, dst) in enumerate(((pos_any, pos_ref), (sl_any, sl_ref), (enc_any, enc_ref)))
    ]
    for load in loads:
        load.start()
    peers = []
    for off in (1, -1, 0):
        for j in range(doms):
            if off == 0 and j == 0:
                continue
            peers.append((off, lax.rem(n + off + groups, groups), lax.rem(me + j, doms)))

    barrier = pltpu.get_barrier_semaphore()
    for _, there, dom in peers:
        pl.semaphore_signal(barrier, inc=1, device_id=(there, dom), device_id_type=MESH)

    for load in loads:
        load.wait()
    centre = 0.5 * (G - 1)
    for beam in range(2):
        gap = sl_ref[beam].astype(F32)
        block[beam * 8 : beam * 8 + 4, :] = (centre + pos_ref[0, beam]) + 4.0 * gap
        block[beam * 8 + 4 : beam * 8 + 8, :] = (centre + pos_ref[1, beam]) + gap
    encs[...] = jnp.zeros_like(encs)
    encs[0:BUN, 0:NOFF] = enc_ref[...]
    pl.semaphore_wait(barrier, len(peers))

    for off in (1, -1):
        pltpu.make_async_remote_copy(
            src_ref=encs,
            dst_ref=e_ref.at[1 - off],
            send_sem=sems.at[0],
            recv_sem=sems.at[1],
            device_id=(lax.rem(n + off + groups, groups), me),
            device_id_type=MESH,
        ).start()
    for off, there, dom in peers:
        pltpu.make_async_remote_copy(
            src_ref=block,
            dst_ref=g_ref.at[(1 - off) * doms + me],
            send_sem=sems.at[2],
            recv_sem=sems.at[3],
            device_id=(there, dom),
            device_id_type=MESH,
        ).start()
    pltpu.make_async_copy(encs, e_ref.at[1], sems.at[1]).start()
    pltpu.make_async_copy(block, g_ref.at[doms + me], sems.at[3]).start()
    for sem, ref in ((3, g_ref), (1, e_ref), (2, g_ref.at[pl.ds(0, len(peers))]), (0, e_ref.at[pl.ds(0, 2)])):
        pltpu.make_async_copy(ref, ref, sems.at[sem]).wait()


def high_low(values):
    high = values.astype(BF)
    return high, (values - high.astype(F32)).astype(BF)


def mm(a, b):
    return jnp.dot(a, b, preferred_element_type=F32)


def live_lists(enc_ref, order, place, pair_c, pair_p, pair_count):
    flags = []
    for beam in range(2):
        for b in range(BUN):
            row = []
            for c in range(NOFF):
                if beam == 0:
                    row.append(enc_ref[1, b, c])
                else:
                    a = b + c + 1
                    row.append(enc_ref[a // BUN, a % BUN, 2 * R - c])
            flags.append(row)
    count = jnp.int32(0)
    for k in range(2 * SRC + 8):
        order[k] = 0
    for source in ALWAYS:
        place[source] = count
        order[count] = source
        count = count + 1
    for source in range(2 * SRC):
        if source in ALWAYS:
            continue
        beam, m = source // SRC, source % SRC
        users = [flags[(1 - beam) * BUN + b][m - b] for b in range(BUN) if 0 <= m - b < NOFF]
        need = users[0]
        for other in users[1:]:
            need = jnp.maximum(need, other)
        order[count] = source
        place[source] = count
        count = count + need
    order[count] = 0
    for target in range(2 * BUN):
        beam, b = target // BUN, target % BUN
        total = jnp.int32(0)
        for c in range(NOFF):
            pair_c[target * 8 + total] = c
            pair_p[target * 8 + total] = place[(1 - beam) * SRC + b + c]
            total = total + flags[target][c]
        pair_count[target] = total
    return count


def solve_kernel(
    doms,
    g_ref, enc_any, fy_any, fx_any, ix_any, iy_any, kv_any,
    f_any, kick_any,
    fy_ref, fx_ref, ix_ref, iy_ref, kv, table_sem,
    wx, wy, grids, spec, acc, bh_ref, bl_ref, win, kick_ref,
    enc_ref, order, place, pair_c, pair_p, pair_count, enc_sem, out_sem,
):
    enc_load = pltpu.make_async_copy(enc_any, enc_ref, enc_sem)
    enc_load.start()
    pairs = ((fy_any, fy_ref), (fx_any, fx_ref), (kv_any, kv), (ix_any, ix_ref), (iy_any, iy_ref))
    loads = [pltpu.make_async_copy(src, dst, table_sem.at[k]) for k, (src, dst) in enumerate(pairs)]
    for load in loads:
        load.start()

    line = lax.broadcasted_iota(jnp.int32, (16, 128), 0).astype(F32)
    lines = [line + 16.0 * t for t in range(ROWS // 16)]

    def weights(source, slot):
        beam = source // SRC
        m = source - beam * SRC
        grp = (m + 1) // BUN
        bunch = (m + 1) % BUN
        for coord, dest in ((0, wx[slot]), (1, wy[slot])):
            row = beam * 8 + coord * 4 + bunch
            for d in range(doms):
                at = jnp.broadcast_to(g_ref[grp * doms + d, pl.ds(row, 1), :], (16, 128))
                cols = slice(d * 128, (d + 1) * 128)
                for t in range(ROWS // 16):
                    high, low = high_low(jnp.maximum(0.0, 1.0 - jnp.abs(at - lines[t])))
                    dest[16 * t : 16 * t + 16, cols] = high
                    dest[ROWS + 16 * t : ROWS + 16 * t + 16, cols] = low

    def deposit(slot):
        both = lax.dot_general(
            wx[slot][...], wy[slot][...], (((1,), (1,)), ((), ())), preferred_element_type=F32
        )
        high, low = high_low(both[:ROWS] + both[ROWS:])
        grids[slot][:ROWS] = high
        grids[slot][ROWS:] = low

    def spectra(k, slots):
        grid = [grids[slot][:ROWS] for slot in slots]
        wide = len(slots) * ROWS
        low = [grids[slot][ROWS:] for slot in slots]
        first = mm(jnp.concatenate(grid + low, axis=0), fy_ref[:, :256])
        first = first[:wide] + first[wide:] + mm(jnp.concatenate(grid, axis=0), fy_ref[:, 256:])
        for s in range(len(slots)):
            high, low = high_low(first[s * ROWS : (s + 1) * ROWS])
            out = mm(fx_ref[...], jnp.concatenate([high, low, high], axis=0))
            cr, ci = out[:ROWS, :128], out[:ROWS, 128:]
            sr, si = out[ROWS:, :128], out[ROWS:, 128:]
            spec[k + s, 0, :ROWS] = cr + si
            spec[k + s, 0, ROWS:] = cr - si
            spec[k + s, 1, :ROWS] = ci - sr
            spec[k + s, 1, ROWS:] = ci + sr

    for s in range(4):
        weights(ALWAYS[s], s)
    enc_load.wait()
    count = live_lists(enc_ref, order, place, pair_c, pair_p, pair_count)
    for s in range(4):
        deposit(s)
        weights(order[4 + s], s)
    for load in loads[:2]:
        load.wait()

    def four_sources(j, _):
        k = 4 * j
        for half in (0, 2):
            spectra(k - 4 + half, (half, half + 1))
        for s in range(4):
            deposit(s)
            weights(order[k + 4 + s], s)
        return 0

    turns = (count + 3) // 4
    lax.fori_loop(1, turns, four_sources, 0)
    for half in (0, 2):
        spectra(4 * turns - 4 + half, (half, half + 1))
    for load in loads[2:]:
        load.wait()

    me = lax.axis_index("dom")
    index = lax.broadcasted_iota(jnp.int32, (ROWS, 128), 0).astype(F32)

    def multiply(target, _):
        def partner(j, add):
            c = pair_c[target * 8 + j]
            p = pair_p[target * 8 + j]
            for t in range(2 * ROWS // 16):
                rows = slice(16 * t, 16 * t + 16)
                re = spec[p, 0, rows]
                im = spec[p, 1, rows]
                for part in range(2):
                    kr = kv[c, part, 0, rows]
                    ki = kv[c, part, 1, rows]
                    real = kr * re - ki * im
                    imag = kr * im + ki * re
                    if add:
                        real = acc[target, part, 0, rows] + real
                        imag = acc[target, part, 1, rows] + imag
                    acc[target, part, 0, rows] = real
                    acc[target, part, 1, rows] = imag

        def later(j, _):
            partner(j, True)
            return 0

        @pl.when(pair_count[target] == 0)
        def _():
            acc[target] = jnp.zeros_like(acc[target])

        @pl.when(pair_count[target] > 0)
        def _():
            partner(0, False)
            lax.fori_loop(1, pair_count[target], later, 0)

        return 0

    lax.fori_loop(0, 2 * BUN, multiply, 0)

    def finish(beam, _):
        for b in range(BUN):
            target = beam * BUN + b
            stacks = []
            for part in range(2):
                rp, rm = acc[target, part, 0, :ROWS], acc[target, part, 0, ROWS:]
                ip, im = acc[target, part, 1, :ROWS], acc[target, part, 1, ROWS:]
                top = jnp.concatenate([rp + rm, ip + im], axis=1)
                low = jnp.concatenate([im - ip, rp - rm], axis=1)
                dh, dl = high_low(jnp.concatenate([top, low], axis=0))
                stacks.append(jnp.concatenate([dh, dl, dh], axis=0))
            first = mm(ix_ref[...], jnp.concatenate(stacks, axis=1))
            for part in range(2):
                rows = slice((2 * b + part) * ROWS, (2 * b + part + 1) * ROWS)
                bh_ref[rows], bl_ref[rows] = high_low(first[:, 256 * part : 256 * part + 256])
        wide = mm(bh_ref[...], iy_ref[...])
        fields = wide[:, :128] + wide[:, 128:] + mm(bl_ref[...], iy_ref[:, :128])
        for b in range(BUN):
            for part in range(2):
                for i in range(SLICES):
                    top = (2 * b + part) * ROWS + 4 * i
                    win[beam, b, i, part] = fields[top : top + G, i : i + G]
        pltpu.make_async_copy(win.at[beam], f_any.at[beam], out_sem.at[beam]).start()
        for b in range(BUN):
            x = jnp.broadcast_to(g_ref[doms + me, pl.ds(beam * 8 + b, 1), :], (ROWS, 128))
            y = jnp.broadcast_to(g_ref[doms + me, pl.ds(beam * 8 + 4 + b, 1), :], (ROWS, 128))
            weight_x = jnp.maximum(0.0, 1.0 - jnp.abs(x - index))
            yh, yl = high_low(jnp.maximum(0.0, 1.0 - jnp.abs(y - index)))
            fh, fl = high_low(fields[2 * b * ROWS : 2 * (b + 1) * ROWS, :ROWS])
            both = mm(jnp.concatenate([fh, fl], axis=0), jnp.concatenate([yh, yl], axis=1))
            sampled = both[: 2 * ROWS, :128] + both[2 * ROWS :, :128] + both[: 2 * ROWS, 128:]
            for part in range(2):
                kick_ref[part, beam, b : b + 1, :] = jnp.sum(
                    weight_x * sampled[part * ROWS : (part + 1) * ROWS], axis=0, keepdims=True
                )
        return 0

    lax.fori_loop(0, 2, finish, 0)
    kicks = pltpu.make_async_copy(kick_ref, kick_any, enc_sem)
    kicks.start()
    for beam in range(2):
        pltpu.make_async_copy(win.at[beam], f_any.at[beam], out_sem.at[beam]).wait()
    kicks.wait()


def solve(gathered, enc):
    doms, particles = gathered.shape[0] // 3, gathered.shape[2]
    vmem = pl.BlockSpec(memory_space=pltpu.VMEM)
    anywhere = pl.BlockSpec(memory_space=pl.ANY)
    consts = [jnp.asarray(t) for t in tables(CHARGE / (particles * doms))]
    weight = pltpu.VMEM((2 * ROWS, doms * particles), BF)
    return pl.pallas_call(
        functools.partial(solve_kernel, doms),
        out_shape=(
            jax.ShapeDtypeStruct((2, BUN, SLICES, 2, G, G), F32),
            jax.ShapeDtypeStruct((2, 2, BUN, particles), F32),
        ),
        in_specs=[vmem] + [anywhere] * (1 + len(consts)),
        out_specs=(anywhere, anywhere),
        scratch_shapes=[pltpu.VMEM(t.shape, t.dtype) for t in consts] + [
            pltpu.SemaphoreType.DMA((len(consts),)),
            [weight] * 4,
            [weight] * 4,
            [pltpu.VMEM((2 * ROWS, 2 * ROWS), BF)] * 4,
            pltpu.VMEM((2 * SRC + 4, 2, 2 * ROWS, 128), F32),
            pltpu.VMEM((2 * BUN, 2, 2, 2 * ROWS, 128), F32),
            pltpu.VMEM((BUN * 2 * ROWS, 256), BF),
            pltpu.VMEM((BUN * 2 * ROWS, 256), BF),
            pltpu.VMEM((2, BUN, SLICES, 2, G, G), F32),
            pltpu.VMEM((2, 2, BUN, particles), F32),
            pltpu.SMEM((3, 8, 128), jnp.int32),
            pltpu.SMEM((2 * SRC + 8,), jnp.int32),
            pltpu.SMEM((2 * SRC,), jnp.int32),
            pltpu.SMEM((2 * BUN * 8,), jnp.int32),
            pltpu.SMEM((2 * BUN * 8,), jnp.int32),
            pltpu.SMEM((2 * BUN,), jnp.int32),
            pltpu.SemaphoreType.DMA,
            pltpu.SemaphoreType.DMA((2,)),
        ],
        compiler_params=pltpu.CompilerParams(vmem_limit_bytes=24 * 1024 * 1024),
        name="solve",
    )(gathered, enc, *[pltpu.with_memory_space_constraint(t, pltpu.HBM) for t in consts])


def on_device(positions, slice_index, encounters):
    groups, doms = lax.axis_size("bunch"), lax.axis_size("dom")
    particles = positions.shape[3]
    anywhere = pl.BlockSpec(memory_space=pl.ANY)
    gathered, enc = pl.pallas_call(
        functools.partial(exchange_kernel, groups, doms),
        out_shape=(
            jax.ShapeDtypeStruct((3 * doms, 16, particles), F32),
            jax.ShapeDtypeStruct((3, 8, 128), jnp.int32),
        ),
        in_specs=[anywhere] * 3,
        out_specs=(anywhere, anywhere),
        scratch_shapes=[
            pltpu.VMEM(positions.shape, F32),
            pltpu.VMEM(slice_index.shape, jnp.int32),
            pltpu.VMEM(encounters.shape, jnp.int32),
            pltpu.VMEM((16, particles), F32),
            pltpu.VMEM((8, 128), jnp.int32),
            pltpu.SemaphoreType.DMA((3,)),
            pltpu.SemaphoreType.DMA((4,)),
        ],
        compiler_params=pltpu.CompilerParams(
            collective_id=0, has_side_effects=True, vmem_limit_bytes=1024 * 1024
        ),
        name="exchange",
    )(*[pltpu.with_memory_space_constraint(v, pltpu.HBM) for v in (positions, slice_index, encounters)])
    return solve(gathered, enc)


def solution(mesh):
    placed = (P(None, None, "bunch", "dom"), P(None, "bunch", "dom"), P("bunch", None))
    return jax.shard_map(
        on_device,
        mesh=mesh,
        in_specs=placed,
        out_specs=(P(None, "bunch", None, None, None, None), P(None, None, "bunch", "dom")),
        check_vma=False,
    )
```

time: 31.3 us -> 31 us (level)
    pallas_call x1, Pallas kernels: 19.5 us -> 18.9 us  [on_device(): pl.pallas_call(functools.partial(exchange_kernel, groups, doms), out_shap...]
where the time goes in v2:
time: 31 us; the launch traced here: 30.8 us
  Pallas kernels  30.2 us (97%)
  between operations  0.64 us (2%)
    pallas_call x1, Pallas kernels, on_device(): pl.pallas_call(functools.partial(exchange_kernel, groups, doms), out_shap...  18.9 us
    pallas_call x1, Pallas kernels, solve(): pl.pallas_call(functools.partial(solve_kernel, doms), out_shape=(jax.Shap...  11.2 us

profile of v2, /device:TPU:3, one launch (start us, length us, event | category | flops | bytes accessed | tf_op | source)
XLA Modules:
  0.0 30.8 jit_solution(10942367226541650844)
XLA Ops:
  0.6 18.9 %exchange.1 = (f32[24,16,128]{2,1,0:T(8,128)S(1)}, s32[3,8,128]{2,1,0:T(8,128)S(1)}) custom-call(f32[2,2,4,128]{3,2,1,0:T(4,128)} %pos_any.1, s32[2,4,128]{2,1,0:T(4,128)} %sl_any.1, s32[4,7]{1,0:T(4,128)} %enc_any.1), custom_call_target="tpu_custom_call" | custom-call | tf_op jit(solution)/shard_map/exchange/pallas_call | solution.py:405
  19.5 11.2 %solve.1 = (f32[2,4,4,2,64,64]{5,4,3,2,1,0:T(8,128)}, f32[2,2,4,128]{3,2,1,0:T(4,128)}) custom-call(f32[24,16,128]{2,1,0:T(8,128)S(1)} %get-tuple-element.4.g_ref, s32[3,8,128]{2,1,0:T(8,128)S(1)} %get-tuple-element.5.enc_any, bf16[160,512]{1,0:T(8,128)(2,1)} %constant.10.clone.fy_any, bf16[160,240]{1,0:T(8,128)(2,1)} %constant.11.clone.fx_any, ...), custom_call_target="tpu_custom_call" | custom-call | tf_op jit(solution)/shard_map/solve/pallas_call | solution.py:368

commit v3 on v2

--- a/solution.py
+++ b/solution.py
@@ -197,7 +197,7 @@
     g_ref, enc_any, fy_any, fx_any, ix_any, iy_any, kv_any,
     f_any, kick_any,
     fy_ref, fx_ref, ix_ref, iy_ref, kv, table_sem,
-    wx, wy, grids, spec, acc, bh_ref, bl_ref, win, kick_ref,
+    q, wx, wy, grids, spec, acc, bh_ref, bl_ref, win, kick_ref,
     enc_ref, order, place, pair_c, pair_p, pair_count, enc_sem, out_sem,
 ):
     enc_load = pltpu.make_async_copy(enc_any, enc_ref, enc_sem)
@@ -207,8 +207,19 @@
     for load in loads:
         load.start()
 
+    where_at = g_ref[...]
+    cell = jnp.floor(where_at)
+    upper = where_at - cell
+    q[0] = cell
+    for slot, part in ((1, 1.0 - upper), (3, upper)):
+        high = part.astype(BF).astype(F32)
+        q[slot] = high
+        q[slot + 1] = part - high
+
     line = lax.broadcasted_iota(jnp.int32, (16, 128), 0).astype(F32)
-    lines = [line + 16.0 * t for t in range(ROWS // 16)]
+    lines = [(line + 16.0 * t).astype(BF) for t in range(ROWS // 16)]
+    below = [(line + (16.0 * t - 1.0)).astype(BF) for t in range(ROWS // 16)]
+    nothing = jnp.zeros((16, 128), BF)
 
     def weights(source, slot):
         beam = source // SRC
@@ -218,12 +229,17 @@
         for coord, dest in ((0, wx[slot]), (1, wy[slot])):
             row = beam * 8 + coord * 4 + bunch
             for d in range(doms):
-                at = jnp.broadcast_to(g_ref[grp * doms + d, pl.ds(row, 1), :], (16, 128))
+                cells, lh, ll, uh, ul = [
+                    jnp.broadcast_to(q[j, grp * doms + d, pl.ds(row, 1), :], (16, 128)).astype(BF) for j in range(5)
+                ]
                 cols = slice(d * 128, (d + 1) * 128)
                 for t in range(ROWS // 16):
-                    high, low = high_low(jnp.maximum(0.0, 1.0 - jnp.abs(at - lines[t])))
-                    dest[16 * t : 16 * t + 16, cols] = high
-                    dest[ROWS + 16 * t : ROWS + 16 * t + 16, cols] = low
+                    first = lines[t] == cells
+                    second = below[t] == cells
+                    dest[16 * t : 16 * t + 16, cols] = jnp.where(first, lh, jnp.where(second, uh, nothing))
+                    dest[ROWS + 16 * t : ROWS + 16 * t + 16, cols] = jnp.where(
+                        first, ll, jnp.where(second, ul, nothing)
+                    )
 
     def deposit(slot):
         both = lax.dot_general(
@@ -375,6 +391,7 @@
         out_specs=(anywhere, anywhere),
         scratch_shapes=[pltpu.VMEM(t.shape, t.dtype) for t in consts] + [
             pltpu.SemaphoreType.DMA((len(consts),)),
+            pltpu.VMEM((5, 3 * doms, 16, particles), F32),
             [weight] * 4,
             [weight] * 4,
             [pltpu.VMEM((2 * ROWS, 2 * ROWS), BF)] * 4,

time: 31 us -> 29.6 us (0.955)
  the two profiles are of different devices: /device:TPU:3 before, /device:TPU:1 now
where the time goes in v3:
time: 29.6 us; the launch traced here: 29.4 us
  Pallas kernels  28.7 us (97%)
  between operations  0.64 us (2%)
    pallas_call x1, Pallas kernels, on_device(): pl.pallas_call(functools.partial(exchange_kernel, groups, doms), out_shap...  20 us
    pallas_call x1, Pallas kernels, solve(): pl.pallas_call(functools.partial(solve_kernel, doms), out_shape=(jax.Shap...  8.71 us

profile of v3, /device:TPU:1, one launch (start us, length us, event | category | flops | bytes accessed | tf_op | source)
XLA Modules:
  0.0 29.4 jit_solution(14617316379127974141)
XLA Ops:
  0.6 20.0 %exchange.1 = (f32[24,16,128]{2,1,0:T(8,128)S(1)}, s32[3,8,128]{2,1,0:T(8,128)S(1)}) custom-call(f32[2,2,4,128]{3,2,1,0:T(4,128)} %pos_any.1, s32[2,4,128]{2,1,0:T(4,128)} %sl_any.1, s32[4,7]{1,0:T(4,128)} %enc_any.1), custom_call_target="tpu_custom_call" | custom-call | tf_op jit(solution)/shard_map/exchange/pallas_call | solution.py:422
  20.7 8.7 %solve.1 = (f32[2,4,4,2,64,64]{5,4,3,2,1,0:T(8,128)}, f32[2,2,4,128]{3,2,1,0:T(4,128)}) custom-call(f32[24,16,128]{2,1,0:T(8,128)S(1)} %get-tuple-element.4.g_ref, s32[3,8,128]{2,1,0:T(8,128)S(1)} %get-tuple-element.5.enc_any, bf16[160,512]{1,0:T(8,128)(2,1)} %constant.10.clone.fy_any, bf16[160,240]{1,0:T(8,128)(2,1)} %constant.11.clone.fx_any, ...), custom_call_target="tpu_custom_call" | custom-call | tf_op jit(solution)/shard_map/solve/pallas_call | solution.py:384

commit v4 on v3

--- a/solution.py
+++ b/solution.py
@@ -44,7 +44,7 @@
     phase_y = 2.0 * np.pi * (line[:, None] * ky[None, :] % N2) / N2
     along = np.concatenate([np.cos(phase_y) * live_ky, -np.sin(phase_y) * live_ky], axis=1)
     high, low = split_table(along)
-    fwd_y = np.concatenate([np.concatenate([high, high], axis=0), np.concatenate([low, low], axis=0)], axis=1)
+    fwd_y = np.concatenate([high, high, low], axis=0)
 
     phase_x = 2.0 * np.pi * (kx[:, None] * line[None, :] % N1) / N1
     cos_x = np.cos(phase_x) * live_kx[:, None]
@@ -245,16 +245,12 @@
         both = lax.dot_general(
             wx[slot][...], wy[slot][...], (((1,), (1,)), ((), ())), preferred_element_type=F32
         )
-        high, low = high_low(both[:ROWS] + both[ROWS:])
-        grids[slot][:ROWS] = high
-        grids[slot][ROWS:] = low
+        both = both[:ROWS] + both[ROWS:]
+        high, low = high_low(both[:, :ROWS] + both[:, ROWS:])
+        grids[slot][...] = jnp.concatenate([high, low, high], axis=1)
 
     def spectra(k, slots):
-        grid = [grids[slot][:ROWS] for slot in slots]
-        wide = len(slots) * ROWS
-        low = [grids[slot][ROWS:] for slot in slots]
-        first = mm(jnp.concatenate(grid + low, axis=0), fy_ref[:, :256])
-        first = first[:wide] + first[wide:] + mm(jnp.concatenate(grid, axis=0), fy_ref[:, 256:])
+        first = mm(jnp.concatenate([grids[slot][...] for slot in slots], axis=0), fy_ref[...])
         for s in range(len(slots)):
             high, low = high_low(first[s * ROWS : (s + 1) * ROWS])
             out = mm(fx_ref[...], jnp.concatenate([high, low, high], axis=0))
@@ -284,10 +280,22 @@
             weights(order[k + 4 + s], s)
         return 0
 
-    turns = (count + 3) // 4
+    turns = (count + 1) // 4
     lax.fori_loop(1, turns, four_sources, 0)
-    for half in (0, 2):
-        spectra(4 * turns - 4 + half, (half, half + 1))
+
+    @pl.when(count > 4 * turns)
+    def _():
+        for half in (0, 2):
+            spectra(4 * turns - 4 + half, (half, half + 1))
+        for s in range(2):
+            deposit(s)
+        spectra(4 * turns, (0, 1))
+
+    @pl.when(count <= 4 * turns)
+    def _():
+        for half in (0, 2):
+            spectra(4 * turns - 4 + half, (half, half + 1))
+
     for load in loads[2:]:
         load.wait()
 
@@ -394,7 +402,7 @@
             pltpu.VMEM((5, 3 * doms, 16, particles), F32),
             [weight] * 4,
             [weight] * 4,
-            [pltpu.VMEM((2 * ROWS, 2 * ROWS), BF)] * 4,
+            [pltpu.VMEM((ROWS, 3 * ROWS), BF)] * 4,
             pltpu.VMEM((2 * SRC + 4, 2, 2 * ROWS, 128), F32),
             pltpu.VMEM((2 * BUN, 2, 2, 2 * ROWS, 128), F32),
             pltpu.VMEM((BUN * 2 * ROWS, 256), BF),

time: 29.6 us -> 29 us (0.980)
  Pallas kernels: 28.7 us -> 28.1 us
    pallas_call x1, Pallas kernels: 8.71 us -> 8.1 us  [solve(): pl.pallas_call(functools.partial(solve_kernel, doms), out_shape=(jax.Shap...]
where the time goes in v4:
time: 29 us; the launch traced here: 28.8 us
  Pallas kernels  28.1 us (97%)
  between operations  0.64 us (2%)
    pallas_call x1, Pallas kernels, on_device(): pl.pallas_call(functools.partial(exchange_kernel, groups, doms), out_shap...  20 us
    pallas_call x1, Pallas kernels, solve(): pl.pallas_call(functools.partial(solve_kernel, doms), out_shape=(jax.Shap...  8.1 us

profile of v4, /device:TPU:1, one launch (start us, length us, event | category | flops | bytes accessed | tf_op | source)
XLA Modules:
  0.0 28.8 jit_solution(7961894497941908052)
XLA Ops:
  0.6 20.0 %exchange.1 = (f32[24,16,128]{2,1,0:T(8,128)S(1)}, s32[3,8,128]{2,1,0:T(8,128)S(1)}) custom-call(f32[2,2,4,128]{3,2,1,0:T(4,128)} %pos_any.1, s32[2,4,128]{2,1,0:T(4,128)} %sl_any.1, s32[4,7]{1,0:T(4,128)} %enc_any.1), custom_call_target="tpu_custom_call" | custom-call | tf_op jit(solution)/shard_map/exchange/pallas_call | solution.py:430
  20.7 8.1 %solve.1 = (f32[2,4,4,2,64,64]{5,4,3,2,1,0:T(8,128)}, f32[2,2,4,128]{3,2,1,0:T(4,128)}) custom-call(f32[24,16,128]{2,1,0:T(8,128)S(1)} %get-tuple-element.4.g_ref, s32[3,8,128]{2,1,0:T(8,128)S(1)} %get-tuple-element.5.enc_any, bf16[240,256]{1,0:T(8,128)(2,1)} %constant.10.clone.fy_any, bf16[160,240]{1,0:T(8,128)(2,1)} %constant.11.clone.fx_any, ...), custom_call_target="tpu_custom_call" | custom-call | tf_op jit(solution)/shard_map/solve/pallas_call | solution.py:392

commit v5 on v4

--- a/solution.py
+++ b/solution.py
@@ -303,37 +303,24 @@
     index = lax.broadcasted_iota(jnp.int32, (ROWS, 128), 0).astype(F32)
 
     def multiply(target, _):
-        def partner(j, add):
-            c = pair_c[target * 8 + j]
-            p = pair_p[target * 8 + j]
-            for t in range(2 * ROWS // 16):
-                rows = slice(16 * t, 16 * t + 16)
-                re = spec[p, 0, rows]
-                im = spec[p, 1, rows]
+        for rows in (slice(0, ROWS), slice(ROWS, 2 * ROWS)):
+
+            def partner(j, sums):
+                c = pair_c[target * 8 + j]
+                p = pair_p[target * 8 + j]
+                re, im = spec[p, 0, rows], spec[p, 1, rows]
+                out = []
                 for part in range(2):
-                    kr = kv[c, part, 0, rows]
-                    ki = kv[c, part, 1, rows]
-                    real = kr * re - ki * im
-                    imag = kr * im + ki * re
-                    if add:
-                        real = acc[target, part, 0, rows] + real
-                        imag = acc[target, part, 1, rows] + imag
-                    acc[target, part, 0, rows] = real
-                    acc[target, part, 1, rows] = imag
-
-        def later(j, _):
-            partner(j, True)
-            return 0
-
-        @pl.when(pair_count[target] == 0)
-        def _():
-            acc[target] = jnp.zeros_like(acc[target])
-
-        @pl.when(pair_count[target] > 0)
-        def _():
-            partner(0, False)
-            lax.fori_loop(1, pair_count[target], later, 0)
-
+                    kr, ki = kv[c, part, 0, rows], kv[c, part, 1, rows]
+                    out.append(sums[2 * part] + (kr * re - ki * im))
+                    out.append(sums[2 * part + 1] + (kr * im + ki * re))
+                return tuple(out)
+
+            zero = jnp.zeros((ROWS, 128), F32)
+            sums = lax.fori_loop(0, pair_count[target], partner, (zero,) * 4)
+            for part in range(2):
+                acc[target, part, 0, rows] = sums[2 * part]
+                acc[target, part, 1, rows] = sums[2 * part + 1]
         return 0
 
     lax.fori_loop(0, 2 * BUN, multiply, 0)

time: 29 us -> 32.2 us (1.11)
  Pallas kernels: 28.1 us -> 31.3 us
    pallas_call x1, Pallas kernels: 8.1 us -> 11.3 us  [solve(): pl.pallas_call(functools.partial(solve_kernel, doms), out_shape=(jax.Shap...]
where the time goes in v5:
time: 32.2 us; the launch traced here: 32 us
  Pallas kernels  31.3 us (97%)
  between operations  0.64 us (2%)
    pallas_call x1, Pallas kernels, on_device(): pl.pallas_call(functools.partial(exchange_kernel, groups, doms), out_shap...  20 us
    pallas_call x1, Pallas kernels, solve(): pl.pallas_call(functools.partial(solve_kernel, doms), out_shape=(jax.Shap...  11.3 us

profile of v5, /device:TPU:1, one launch (start us, length us, event | category | flops | bytes accessed | tf_op | source)
XLA Modules:
  0.0 32.0 jit_solution(7789832464042720717)
XLA Ops:
  0.6 20.0 %exchange.1 = (f32[24,16,128]{2,1,0:T(8,128)S(1)}, s32[3,8,128]{2,1,0:T(8,128)S(1)}) custom-call(f32[2,2,4,128]{3,2,1,0:T(4,128)} %pos_any.1, s32[2,4,128]{2,1,0:T(4,128)} %sl_any.1, s32[4,7]{1,0:T(4,128)} %enc_any.1), custom_call_target="tpu_custom_call" | custom-call | tf_op jit(solution)/shard_map/exchange/pallas_call | solution.py:417
  20.7 11.3 %solve.1 = (f32[2,4,4,2,64,64]{5,4,3,2,1,0:T(8,128)}, f32[2,2,4,128]{3,2,1,0:T(4,128)}) custom-call(f32[24,16,128]{2,1,0:T(8,128)S(1)} %get-tuple-element.4.g_ref, s32[3,8,128]{2,1,0:T(8,128)S(1)} %get-tuple-element.5.enc_any, bf16[240,256]{1,0:T(8,128)(2,1)} %constant.10.clone.fy_any, bf16[160,240]{1,0:T(8,128)(2,1)} %constant.11.clone.fx_any, ...), custom_call_target="tpu_custom_call" | custom-call | tf_op jit(solution)/shard_map/solve/pallas_call | solution.py:379

commit v6 on v4

--- a/solution.py
+++ b/solution.py
@@ -197,7 +197,7 @@
     g_ref, enc_any, fy_any, fx_any, ix_any, iy_any, kv_any,
     f_any, kick_any,
     fy_ref, fx_ref, ix_ref, iy_ref, kv, table_sem,
-    q, wx, wy, grids, spec, acc, bh_ref, bl_ref, win, kick_ref,
+    wx, wy, grids, spec, acc, bh_ref, bl_ref, win, kick_ref,
     enc_ref, order, place, pair_c, pair_p, pair_count, enc_sem, out_sem,
 ):
     enc_load = pltpu.make_async_copy(enc_any, enc_ref, enc_sem)
@@ -207,15 +207,6 @@
     for load in loads:
         load.start()
 
-    where_at = g_ref[...]
-    cell = jnp.floor(where_at)
-    upper = where_at - cell
-    q[0] = cell
-    for slot, part in ((1, 1.0 - upper), (3, upper)):
-        high = part.astype(BF).astype(F32)
-        q[slot] = high
-        q[slot + 1] = part - high
-
     line = lax.broadcasted_iota(jnp.int32, (16, 128), 0).astype(F32)
     lines = [(line + 16.0 * t).astype(BF) for t in range(ROWS // 16)]
     below = [(line + (16.0 * t - 1.0)).astype(BF) for t in range(ROWS // 16)]
@@ -229,9 +220,12 @@
         for coord, dest in ((0, wx[slot]), (1, wy[slot])):
             row = beam * 8 + coord * 4 + bunch
             for d in range(doms):
-                cells, lh, ll, uh, ul = [
-                    jnp.broadcast_to(q[j, grp * doms + d, pl.ds(row, 1), :], (16, 128)).astype(BF) for j in range(5)
-                ]
+                at = jnp.broadcast_to(g_ref[grp * doms + d, pl.ds(row, 1), :], (8, 128))
+                cell = jnp.floor(at)
+                upper = at - cell
+                lower = 1.0 - upper
+                values = [cell, lower, lower - lower.astype(BF).astype(F32), upper, upper - upper.astype(BF).astype(F32)]
+                cells, lh, ll, uh, ul = [jnp.concatenate([v, v], axis=0).astype(BF) for v in values]
                 cols = slice(d * 128, (d + 1) * 128)
                 for t in range(ROWS // 16):
                     first = lines[t] == cells
@@ -249,11 +243,15 @@
         high, low = high_low(both[:, :ROWS] + both[:, ROWS:])
         grids[slot][...] = jnp.concatenate([high, low, high], axis=1)
 
-    def spectra(k, slots):
-        first = mm(jnp.concatenate([grids[slot][...] for slot in slots], axis=0), fy_ref[...])
-        for s in range(len(slots)):
+    def along_y(slots):
+        return mm(jnp.concatenate([grids[slot][...] for slot in slots], axis=0), fy_ref[...])
+
+    def along_x(k, first):
+        outs = []
+        for s in range(first.shape[0] // ROWS):
             high, low = high_low(first[s * ROWS : (s + 1) * ROWS])
-            out = mm(fx_ref[...], jnp.concatenate([high, low, high], axis=0))
+            outs.append(mm(fx_ref[...], jnp.concatenate([high, low, high], axis=0)))
+        for s, out in enumerate(outs):
             cr, ci = out[:ROWS, :128], out[:ROWS, 128:]
             sr, si = out[ROWS:, :128], out[ROWS:, 128:]
             spec[k + s, 0, :ROWS] = cr + si
@@ -273,11 +271,15 @@
 
     def four_sources(j, _):
         k = 4 * j
-        for half in (0, 2):
-            spectra(k - 4 + half, (half, half + 1))
-        for s in range(4):
+        first, second = along_y((0, 1)), along_y((2, 3))
+        for s in range(2):
             deposit(s)
             weights(order[k + 4 + s], s)
+        along_x(k - 4, first)
+        for s in range(2, 4):
+            deposit(s)
+            weights(order[k + 4 + s], s)
+        along_x(k - 2, second)
         return 0
 
     turns = (count + 1) // 4
@@ -285,16 +287,19 @@
 
     @pl.when(count > 4 * turns)
     def _():
-        for half in (0, 2):
-            spectra(4 * turns - 4 + half, (half, half + 1))
+        first, second = along_y((0, 1)), along_y((2, 3))
         for s in range(2):
             deposit(s)
-        spectra(4 * turns, (0, 1))
+        along_x(4 * turns - 4, first)
+        third = along_y((0, 1))
+        along_x(4 * turns - 2, second)
+        along_x(4 * turns, third)
 
     @pl.when(count <= 4 * turns)
     def _():
-        for half in (0, 2):
-            spectra(4 * turns - 4 + half, (half, half + 1))
+        first, second = along_y((0, 1)), along_y((2, 3))
+        along_x(4 * turns - 4, first)
+        along_x(4 * turns - 2, second)
 
     for load in loads[2:]:
         load.wait()
@@ -339,6 +344,7 @@
     lax.fori_loop(0, 2 * BUN, multiply, 0)
 
     def finish(beam, _):
+        firsts = []
         for b in range(BUN):
             target = beam * BUN + b
             stacks = []
@@ -349,7 +355,8 @@
                 low = jnp.concatenate([im - ip, rp - rm], axis=1)
                 dh, dl = high_low(jnp.concatenate([top, low], axis=0))
                 stacks.append(jnp.concatenate([dh, dl, dh], axis=0))
-            first = mm(ix_ref[...], jnp.concatenate(stacks, axis=1))
+            firsts.append(mm(ix_ref[...], jnp.concatenate(stacks, axis=1)))
+        for b, first in enumerate(firsts):
             for part in range(2):
                 rows = slice((2 * b + part) * ROWS, (2 * b + part + 1) * ROWS)
                 bh_ref[rows], bl_ref[rows] = high_low(first[:, 256 * part : 256 * part + 256])
@@ -360,14 +367,16 @@
                 for i in range(SLICES):
                     top = (2 * b + part) * ROWS + 4 * i
                     win[beam, b, i, part] = fields[top : top + G, i : i + G]
-        pltpu.make_async_copy(win.at[beam], f_any.at[beam], out_sem.at[beam]).start()
+            pltpu.make_async_copy(win.at[beam, b], f_any.at[beam, b], out_sem.at[beam]).start()
+        products = []
         for b in range(BUN):
-            x = jnp.broadcast_to(g_ref[doms + me, pl.ds(beam * 8 + b, 1), :], (ROWS, 128))
             y = jnp.broadcast_to(g_ref[doms + me, pl.ds(beam * 8 + 4 + b, 1), :], (ROWS, 128))
-            weight_x = jnp.maximum(0.0, 1.0 - jnp.abs(x - index))
             yh, yl = high_low(jnp.maximum(0.0, 1.0 - jnp.abs(y - index)))
             fh, fl = high_low(fields[2 * b * ROWS : 2 * (b + 1) * ROWS, :ROWS])
-            both = mm(jnp.concatenate([fh, fl], axis=0), jnp.concatenate([yh, yl], axis=1))
+            products.append(mm(jnp.concatenate([fh, fl], axis=0), jnp.concatenate([yh, yl], axis=1)))
+        for b, both in enumerate(products):
+            x = jnp.broadcast_to(g_ref[doms + me, pl.ds(beam * 8 + b, 1), :], (ROWS, 128))
+            weight_x = jnp.maximum(0.0, 1.0 - jnp.abs(x - index))
             sampled = both[: 2 * ROWS, :128] + both[2 * ROWS :, :128] + both[: 2 * ROWS, 128:]
             for part in range(2):
                 kick_ref[part, beam, b : b + 1, :] = jnp.sum(
@@ -399,7 +408,6 @@
         out_specs=(anywhere, anywhere),
         scratch_shapes=[pltpu.VMEM(t.shape, t.dtype) for t in consts] + [
             pltpu.SemaphoreType.DMA((len(consts),)),
-            pltpu.VMEM((5, 3 * doms, 16, particles), F32),
             [weight] * 4,
             [weight] * 4,
             [pltpu.VMEM((ROWS, 3 * ROWS), BF)] * 4,

time: 29 us -> 27.8 us (0.959)
  the two profiles are of different devices: /device:TPU:1 before, /device:TPU:3 now
where the time goes in v6:
time: 27.8 us; the launch traced here: 27.6 us
  Pallas kernels  27 us (97%)
  between operations  0.64 us (2%)
    pallas_call x1, Pallas kernels, on_device(): pl.pallas_call(functools.partial(exchange_kernel, groups, doms), out_shap...  18.9 us
    pallas_call x1, Pallas kernels, solve(): pl.pallas_call(functools.partial(solve_kernel, doms), out_shape=(jax.Shap...  8.06 us

profile of v6, /device:TPU:3, one launch (start us, length us, event | category | flops | bytes accessed | tf_op | source)
XLA Modules:
  0.0 27.6 jit_solution(1604202373536684800)
XLA Ops:
  0.6 18.9 %exchange.1 = (f32[24,16,128]{2,1,0:T(8,128)S(1)}, s32[3,8,128]{2,1,0:T(8,128)S(1)}) custom-call(f32[2,2,4,128]{3,2,1,0:T(4,128)} %pos_any.1, s32[2,4,128]{2,1,0:T(4,128)} %sl_any.1, s32[4,7]{1,0:T(4,128)} %enc_any.1), custom_call_target="tpu_custom_call" | custom-call | tf_op jit(solution)/shard_map/exchange/pallas_call | solution.py:438
  19.5 8.1 %solve.1 = (f32[2,4,4,2,64,64]{5,4,3,2,1,0:T(8,128)}, f32[2,2,4,128]{3,2,1,0:T(4,128)}) custom-call(f32[24,16,128]{2,1,0:T(8,128)S(1)} %get-tuple-element.4.g_ref, s32[3,8,128]{2,1,0:T(8,128)S(1)} %get-tuple-element.5.enc_any, bf16[240,256]{1,0:T(8,128)(2,1)} %constant.10.clone.fy_any, bf16[160,240]{1,0:T(8,128)(2,1)} %constant.11.clone.fx_any, ...), custom_call_target="tpu_custom_call" | custom-call | tf_op jit(solution)/shard_map/solve/pallas_call | solution.py:401

commit v7 on v6

--- a/solution.py
+++ b/solution.py
@@ -263,23 +263,27 @@
         weights(ALWAYS[s], s)
     enc_load.wait()
     count = live_lists(enc_ref, order, place, pair_c, pair_p, pair_count)
-    for s in range(4):
+    deposit(0)
+    for s in range(1, 4):
         deposit(s)
-        weights(order[4 + s], s)
+        weights(order[3 + s], s - 1)
+    weights(order[7], 3)
     for load in loads[:2]:
         load.wait()
 
     def four_sources(j, _):
         k = 4 * j
         first, second = along_y((0, 1)), along_y((2, 3))
-        for s in range(2):
-            deposit(s)
-            weights(order[k + 4 + s], s)
+        deposit(0)
+        deposit(1)
+        weights(order[k + 4], 0)
         along_x(k - 4, first)
-        for s in range(2, 4):
-            deposit(s)
-            weights(order[k + 4 + s], s)
+        deposit(2)
+        weights(order[k + 5], 1)
+        deposit(3)
+        weights(order[k + 6], 2)
         along_x(k - 2, second)
+        weights(order[k + 7], 3)
         return 0
 
     turns = (count + 1) // 4
@@ -311,10 +315,11 @@
         def partner(j, add):
             c = pair_c[target * 8 + j]
             p = pair_p[target * 8 + j]
-            for t in range(2 * ROWS // 16):
-                rows = slice(16 * t, 16 * t + 16)
+            for t in range(2 * ROWS // 32):
+                rows = slice(32 * t, 32 * t + 32)
                 re = spec[p, 0, rows]
                 im = spec[p, 1, rows]
+                sums = []
                 for part in range(2):
                     kr = kv[c, part, 0, rows]
                     ki = kv[c, part, 1, rows]
@@ -323,8 +328,9 @@
                     if add:
                         real = acc[target, part, 0, rows] + real
                         imag = acc[target, part, 1, rows] + imag
-                    acc[target, part, 0, rows] = real
-                    acc[target, part, 1, rows] = imag
+                    sums += [real, imag]
+                for place, value in enumerate(sums):
+                    acc[target, place // 2, place % 2, rows] = value
 
         def later(j, _):
             partner(j, True)

time: 27.8 us -> 28.3 us (1.018)
  the two profiles are of different devices: /device:TPU:3 before, /device:TPU:1 now
where the time goes in v7:
time: 28.3 us; the launch traced here: 28.8 us
  Pallas kernels  28.1 us (99%)
  between operations  0.64 us (2%)
    pallas_call x1, Pallas kernels, on_device(): pl.pallas_call(functools.partial(exchange_kernel, groups, doms), out_shap...  20 us
    pallas_call x1, Pallas kernels, solve(): pl.pallas_call(functools.partial(solve_kernel, doms), out_shape=(jax.Shap...  8.08 us

profile of v7, /device:TPU:1, one launch (start us, length us, event | category | flops | bytes accessed | tf_op | source)
XLA Modules:
  0.0 28.8 jit_solution(7531243871473589169)
XLA Ops:
  0.6 20.0 %exchange.1 = (f32[24,16,128]{2,1,0:T(8,128)S(1)}, s32[3,8,128]{2,1,0:T(8,128)S(1)}) custom-call(f32[2,2,4,128]{3,2,1,0:T(4,128)} %pos_any.1, s32[2,4,128]{2,1,0:T(4,128)} %sl_any.1, s32[4,7]{1,0:T(4,128)} %enc_any.1), custom_call_target="tpu_custom_call" | custom-call | tf_op jit(solution)/shard_map/exchange/pallas_call | solution.py:444
  20.7 8.1 %solve.1 = (f32[2,4,4,2,64,64]{5,4,3,2,1,0:T(8,128)}, f32[2,2,4,128]{3,2,1,0:T(4,128)}) custom-call(f32[24,16,128]{2,1,0:T(8,128)S(1)} %get-tuple-element.4.g_ref, s32[3,8,128]{2,1,0:T(8,128)S(1)} %get-tuple-element.5.enc_any, bf16[240,256]{1,0:T(8,128)(2,1)} %constant.10.clone.fy_any, bf16[160,240]{1,0:T(8,128)(2,1)} %constant.11.clone.fx_any, ...), custom_call_target="tpu_custom_call" | custom-call | tf_op jit(solution)/shard_map/solve/pallas_call | solution.py:407
